TPU v7x, 128 devices: a whole 4x4x4 slice. The times are simulated.
128 devices in a mesh: dp: 8 (over y, core), tensor: 16 (over z, x).
Axes of the slice: x: 4, y: 4, z: 4, core: 2. Of those that a mesh axis runs over, the one named last changes fastest.
Arguments:
- tokens: bfloat16 [16384, 8192], P('dp', 'tensor'), may hold values from -6 to 6
- cotangent: bfloat16 [16384, 8192], P('dp', 'tensor'), may hold values from -6 to 6
- first_blocks: bfloat16 [32, 256, 256], P('tensor'), may hold values from -0.375 to 0.375
- second_blocks: bfloat16 [32, 256, 1024], P('tensor'), may hold values from -0.375 to 0.375
- third_blocks: bfloat16 [32, 1024, 256], P('tensor'), may hold values from -0.1875 to 0.1875
- fourth_blocks: bfloat16 [32, 256, 256], P('tensor'), may hold values from -0.375 to 0.375
Outputs:
- layer_out: bfloat16 [16384, 8192], P('dp', 'tensor')
- tokens_grad: bfloat16 [16384, 8192], P('dp', 'tensor')
- first_grad: float32 [32, 256, 256], P('tensor', 'dp')
- second_grad: float32 [32, 256, 1024], P('tensor', 'dp')
- third_grad: float32 [32, 1024, 256], P('tensor', 'dp')
- fourth_grad: float32 [32, 256, 256], P('tensor', 'dp')
All inputs are finite; a program needn't handle non-finite values.
Results may differ from a plain program's by a relative error of at most 0.017.
Values may be sent and summed in bfloat16 or wider, within the bound.
A program may use at most 128 MiB of HBM per device.

v0:
```python
import jax
import jax.numpy as jnp
from jax import lax
from jax.sharding import PartitionSpec as P


def permute(slots):
    return lax.all_to_all(slots, "tensor", split_axis=0, concat_axis=0, tiled=True)


def shards(tokens, cotangent, first_blocks, second_blocks, third_blocks, fourth_blocks):
    group_size = lax.axis_size("tensor")
    local_blocks = first_blocks.shape[0]
    block_width = first_blocks.shape[1]
    hidden_width = second_blocks.shape[2]
    row_count = tokens.shape[0]
    total_blocks = local_blocks * group_size
    sub_width = block_width // total_blocks
    piece_width = local_blocks * sub_width
    scale_factor = (row_count * lax.axis_size("dp")) ** (-0.5)
    single = jnp.float32
    inputs = tokens.reshape(row_count, local_blocks, block_width)
    first_view = first_blocks.reshape(local_blocks, block_width, group_size, piece_width)
    mixed_in = jnp.einsum(
        "trc,rcqp->qrpt", inputs, first_view, preferred_element_type=single
    ).astype(jnp.bfloat16)
    arrived = permute(mixed_in)
    arrived_view = arrived.reshape(group_size, local_blocks, local_blocks, sub_width, row_count)
    second_view = second_blocks.reshape(
        local_blocks, sub_width, group_size, local_blocks, hidden_width
    )
    pre_act = jnp.einsum(
        "qakst,ksqao->tko", arrived_view, second_view, preferred_element_type=single
    )
    hidden = jax.nn.gelu(pre_act).astype(jnp.bfloat16)
    third_view = third_blocks.reshape(local_blocks, hidden_width, group_size, piece_width)
    down_slots = jnp.einsum(
        "tko,koqp->qkpt", hidden, third_view, preferred_element_type=single
    ).astype(jnp.bfloat16)
    returned = permute(down_slots)
    returned_view = returned.reshape(group_size, local_blocks, local_blocks, sub_width, row_count)
    fourth_view = fourth_blocks.reshape(
        local_blocks, sub_width, group_size, local_blocks, block_width
    )
    layer_out = jnp.einsum(
        "qalst,lsqac->tlc", returned_view, fourth_view, preferred_element_type=single
    )
    layer_out = layer_out.astype(jnp.bfloat16).reshape(row_count, local_blocks * block_width)
    grads_in = cotangent.reshape(row_count, local_blocks, block_width)
    back_slots = jnp.einsum(
        "tlc,lsqac->qalst", grads_in, fourth_view, preferred_element_type=single
    ).astype(jnp.bfloat16)
    back_slots = back_slots.reshape(group_size, local_blocks, piece_width, row_count)
    fourth_part = jnp.einsum(
        "qalst,tlc->lsqac", returned_view, grads_in, preferred_element_type=single
    )
    fourth_part = fourth_part.reshape(local_blocks, block_width, block_width) * scale_factor
    back_down = permute(back_slots)
    third_part = jnp.einsum("tko,qkpt->koqp", hidden, back_down, preferred_element_type=single)
    third_part = third_part.reshape(local_blocks, hidden_width, block_width) * scale_factor
    hidden_grad = jnp.einsum("qkpt,koqp->tko", back_down, third_view, preferred_element_type=single)
    unused, pull_back = jax.vjp(jax.nn.gelu, pre_act)
    pre_grad = pull_back(hidden_grad)[0].astype(jnp.bfloat16)
    fourth_grad, third_grad = (
        lax.psum_scatter(
            fourth_part.astype(jnp.bfloat16), "dp", scatter_dimension=1, tiled=True
        ).astype(jnp.float32),
        lax.psum_scatter(
            third_part.astype(jnp.bfloat16), "dp", scatter_dimension=1, tiled=True
        ).astype(jnp.float32),
    )
    second_part = jnp.einsum(
        "qakst,tko->ksqao", arrived_view, pre_grad, preferred_element_type=single
    )
    second_part = second_part.reshape(local_blocks, block_width, hidden_width) * scale_factor
    middle_slots = jnp.einsum(
        "tko,ksqao->qakst", pre_grad, second_view, preferred_element_type=single
    ).astype(jnp.bfloat16)
    middle_slots = middle_slots.reshape(group_size, local_blocks, piece_width, row_count)
    back_first = permute(middle_slots)
    first_part = jnp.einsum("trc,qrpt->rcqp", inputs, back_first, preferred_element_type=single)
    first_part = first_part.reshape(local_blocks, block_width, block_width) * scale_factor
    tokens_grad = jnp.einsum(
        "qrpt,rcqp->trc", back_first, first_view, preferred_element_type=single
    )
    tokens_grad = tokens_grad.astype(jnp.bfloat16).reshape(row_count, local_blocks * block_width)
    first_grad, second_grad = (
        lax.psum_scatter(
            first_part.astype(jnp.bfloat16), "dp", scatter_dimension=1, tiled=True
        ).astype(jnp.float32),
        lax.psum_scatter(
            second_part.astype(jnp.bfloat16), "dp", scatter_dimension=1, tiled=True
        ).astype(jnp.float32),
    )
    return (layer_out, tokens_grad, first_grad, second_grad, third_grad, fourth_grad)


def solution(mesh):
    in_specs = (
        P("dp", "tensor"),
        P("dp", "tensor"),
        P("tensor", None, None),
        P("tensor", None, None),
        P("tensor", None, None),
        P("tensor", None, None),
    )
    out_specs = (
        P("dp", "tensor"),
        P("dp", "tensor"),
        P("tensor", "dp", None),
        P("tensor", "dp", None),
        P("tensor", "dp", None),
        P("tensor", "dp", None),
    )
    return jax.shard_map(shards, mesh=mesh, in_specs=in_specs, out_specs=out_specs, check_vma=False)
```

profile of v0, /device:TPU:1, one launch (start us, length us, event | category | flops | bytes accessed | tf_op | source)
XLA Modules:
  0.0 256.5 jit_solution(15242077976796196611)
XLA Ops:
  7.2 2.6 %reshape.65 = bf16[2048,2,256]{2,1,0:T(2,128)(2,1)S(1)} reshape(bf16[2048,512]{1,0:T(8,128)(2,1)} %param.6) | data formatting | bytes 4194304 | tf_op jit(solution)/shard_map/reshape | solution.py:22
  11.2 1.5 copy.127
  12.6 8.6 %all-to-all-start = ((bf16[16,2,16,2048]{3,2,1,0:T(8,128)(2,1)}), bf16[16,2,16,2048]{3,2,1,0:T(8,128)(2,1)}, u32[]{:S(2)}, u32[]{:S(2)}) async-start(bf16[16,2,16,2048]{3,2,1,0:T(8,128)(2,1)} %copy.127), calls=%async_computation | async-start | bytes 4194304 | tf_op jit(solution)/shard_map/all_to_all | solution.py:8
  21.3 1.2 reshape.67
  22.5 2.6 %reshape.72 = bf16[2048,2,256]{2,1,0:T(2,128)(2,1)S(1)} reshape(bf16[2048,512]{1,0:T(8,128)(2,1)} %param.7) | data formatting | bytes 4194304 | tf_op jit(solution)/shard_map/reshape | solution.py:49
  26.5 2.5 copy.136
  29.0 1.3 copy.130
  30.3 21.5 %all-to-all-done = bf16[16,2,16,2048]{3,2,1,0:T(8,128)(2,1)} async-done(((bf16[16,2,16,2048]{3,2,1,0:T(8,128)(2,1)}), bf16[16,2,16,2048]{3,2,1,0:T(8,128)(2,1)}, u32[]{:S(2)}, u32[]{:S(2)}) %all-to-all-start) | async-done | bytes 2097184 | tf_op jit(solution)/shard_map/all_to_all | solution.py:8
  51.8 4.3 %all-to-all-start.2 = ((bf16[16,2,16,2048]{3,2,1,0:T(8,128)(2,1)}), bf16[16,2,16,2048]{3,2,1,0:T(8,128)(2,1)S(1)}, u32[]{:S(2)}, u32[]{:S(2)}) async-start(bf16[16,2,16,2048]{3,2,1,0:T(8,128)(2,1)} %copy.136), calls=%async_computation.2 | async-start | bytes 4194304 | tf_op jit(solution)/shard_map/all_to_all | solution.py:8
  56.1 13.5 %fusion.10 = (bf16[2048,2,1024]{2,0,1:T(8,128)(2,1)}, f32[2,2048,1024,1,1]{2,1,0,4,3:T(8,128)}) fusion(bf16[2,8,16,2,1024]{4,3,2,1,0:T(2,128)(2,1)} %reshape.67, bf16[16,2,16,2048]{3,2,1,0:T(8,128)(2,1)} %all-to-all-done), kind=kOutput, calls=%fused_computation.15 | convolution fusion | flops 2185232384 | bytes 28311552 | tf_op jit(solution)/shard_map/qakst,ksqao->tko/dot_general | solution.py:32
  69.6 15.2 %all-to-all-done.2 = bf16[16,2,16,2048]{3,2,1,0:T(8,128)(2,1)S(1)} async-done(((bf16[16,2,16,2048]{3,2,1,0:T(8,128)(2,1)}), bf16[16,2,16,2048]{3,2,1,0:T(8,128)(2,1)S(1)}, u32[]{:S(2)}, u32[]{:S(2)}) %all-to-all-start.2) | async-done | bytes 2097184 | tf_op jit(solution)/shard_map/all_to_all | solution.py:8
  84.8 17.2 %fusion.6 = bf16[2048,2,1024]{2,0,1:T(8,128)(2,1)} fusion(f32[2,2048,1024,1,1]{2,1,0,4,3:T(8,128)} %get-tuple-element.40, bf16[16,2,16,2048]{3,2,1,0:T(8,128)(2,1)S(1)} %all-to-all-done.2, bf16[2,1024,16,16]{1,3,2,0:T(8,128)(2,1)} %bitcast.124), kind=kOutput, calls=%fused_computation.8 | convolution fusion | flops 2231369728 | bytes 28311552 | tf_op jit(solution)/shard_map/qkpt,koqp->tko/dot_general | solution.py:61
  102.0 5.8 %fusion.17 = bf16[2,2048,8,16,2]{1,3,4,2,0:T(8,128)(2,1)S(1)} fusion(bf16[2048,2,1024]{2,0,1:T(8,128)(2,1)} %fusion.6, bf16[2,8,16,2,1024]{4,3,2,1,0:T(2,128)(2,1)S(1)} %copy-done.15), kind=kOutput, calls=%fused_computation.26 | convolution fusion | flops 2148532224 | bytes 11534336 | tf_op jit(solution)/shard_map/tko,ksqao->qakst/dot_general | solution.py:76
  107.8 2.5 copy.139
  110.3 5.5 %all-to-all-start.3 = ((bf16[16,2,16,2048]{3,2,1,0:T(8,128)(2,1)}), bf16[16,2,16,2048]{3,2,1,0:T(8,128)(2,1)S(1)}, u32[]{:S(2)}, u32[]{:S(2)}) async-start(bf16[16,2,16,2048]{3,2,1,0:T(8,128)(2,1)} %copy.139), calls=%async_computation.3 | async-start | bytes 4194304 | tf_op jit(solution)/shard_map/all_to_all | solution.py:8
  116.0 5.8 %fusion.80 = f32[2,2048,256]{1,2,0:S(1)} fusion(bf16[2048,2,1024]{2,0,1:T(8,128)(2,1)} %get-tuple-element.39, bf16[2,1024,256]{2,1,0:T(8,128)(2,1)S(1)} %copy-done.14), kind=kOutput, calls=%fused_computation.61 | convolution fusion | flops 2147483648 | bytes 13631488
  122.1 1.5 copy.131
  124.4 5.7 %multiply_convert_fusion = bf16[2,1024,16,16]{1,3,2,0:T(8,128)(2,1)S(1)} fusion(bf16[16,2,16,2048]{3,2,1,0:T(8,128)(2,1)S(1)} %copy-done.12, bf16[2048,2,1024]{2,0,1:T(8,128)(2,1)} %get-tuple-element.39), kind=kOutput, calls=%fused_computation.39 | convolution fusion | flops 2148532224 | bytes 11534336 | tf_op jit(solution)/shard_map/tko,qkpt->koqp/dot_general | solution.py:59
  130.1 1.3 copy.147
  131.5 13.8 %all-to-all-done.3 = bf16[16,2,16,2048]{3,2,1,0:T(8,128)(2,1)S(1)} async-done(((bf16[16,2,16,2048]{3,2,1,0:T(8,128)(2,1)}), bf16[16,2,16,2048]{3,2,1,0:T(8,128)(2,1)S(1)}, u32[]{:S(2)}, u32[]{:S(2)}) %all-to-all-start.3) | async-done | bytes 2097184 | tf_op jit(solution)/shard_map/all_to_all | solution.py:8
  145.3 1.3 copy-done.4
  146.6 4.9 %all-to-all-start.1 = ((bf16[16,2,16,2048]{3,2,1,0:T(8,128)(2,1)}), bf16[16,2,16,2048]{3,2,1,0:T(8,128)(2,1)}, u32[]{:S(2)}, u32[]{:S(2)}) async-start(bf16[16,2,16,2048]{3,2,1,0:T(8,128)(2,1)} %copy.131), calls=%async_computation.1 | async-start | bytes 4194304 | tf_op jit(solution)/shard_map/all_to_all | solution.py:8
  151.6 6.7 %fusion.44 = bf16[2,8,16,2,1024]{4,2,1,3,0:T(8,128)(2,1)S(1)} fusion(bf16[16,2,2,8,2048]{4,3,2,1,0:T(8,128)(2,1)} %bitcast.35, bf16[2048,2,1024]{2,0,1:T(8,128)(2,1)} %fusion.6), kind=kOutput, calls=%fused_computation.46 | convolution fusion | flops 2148532224 | bytes 11534336 | tf_op jit(solution)/shard_map/qakst,tko->ksqao/dot_general | solution.py:72
  158.3 2.1 copy.145
  162.0 16.9 %all-to-all-done.1 = bf16[16,2,16,2048]{3,2,1,0:T(8,128)(2,1)} async-done(((bf16[16,2,16,2048]{3,2,1,0:T(8,128)(2,1)}), bf16[16,2,16,2048]{3,2,1,0:T(8,128)(2,1)}, u32[]{:S(2)}, u32[]{:S(2)}) %all-to-all-start.1) | async-done | bytes 2097184 | tf_op jit(solution)/shard_map/all_to_all | solution.py:8
  178.9 2.4 fusion.69
  183.5 2.1 bitcast_convert_fusion.1
  185.6 4.0 %copy.152 = bf16[2048,512]{1,0:T(8,128)(2,1)} copy(bf16[2048,512]{0,1:T(8,128)(2,1)} %bitcast.116) | data formatting | bytes 4194304
  189.6 2.4 bitcast_convert_fusion
  192.0 2.5 copy.151
  194.5 1.6 convert_element_type.111
  196.1 49.6 %all-reduce.6.cloned.1.call-done = (bf16[2,256,256]{2,0,1:T(2,128)(2,1)}, bf16[2,256,1024]{2,0,1:T(2,128)(2,1)}, bf16[2,256,256]{2,0,1:T(2,128)(2,1)}) async-done(((bf16[2,256,256]{2,0,1:T(2,128)(2,1)}, bf16[2,256,1024]{2,0,1:T(2,128)(2,1)}, bf16[2,256,256]{2,0,1:T(2,128)(2,1)}), (bf16[2,256,256]{2,0,1:T(2,128)(2,1)}, bf16[2,256,1024]{2,0,1:T(2,128)(2,1)}, ...) | async-done | bytes 1572880
  (56 shorter events, 11.4 us)
Async XLA Ops:
  7.2 2.6 %copy-start.16 = (bf16[2,256,256]{2,1,0:T(8,128)(2,1)S(1)}, bf16[2,256,256]{2,1,0:T(8,128)(2,1)}, u32[]{:S(2)}) copy-start(bf16[2,256,256]{2,1,0:T(8,128)(2,1)} %param.8) | copy-start | bytes 786436
  9.8 1.3 copy-start
  9.9 1.2 copy-start.7
  12.6 8.6 %copy-start.13 = (bf16[2,256,1024]{2,1,0:T(8,128)(2,1)S(1)}, bf16[2,256,1024]{2,1,0:T(8,128)(2,1)}, u32[]{:S(2)}) copy-start(bf16[2,256,1024]{2,1,0:T(8,128)(2,1)} %param.9) | copy-start | bytes 3145732
  12.6 39.2 %all-to-all-start = ((bf16[16,2,16,2048]{3,2,1,0:T(8,128)(2,1)}), bf16[16,2,16,2048]{3,2,1,0:T(8,128)(2,1)}, u32[]{:S(2)}, u32[]{:S(2)}) async-start(bf16[16,2,16,2048]{3,2,1,0:T(8,128)(2,1)} %copy.127), calls=%async_computation | async-start | bytes 4194304 | tf_op jit(solution)/shard_map/all_to_all | solution.py:8
  22.5 2.6 %copy-start.17 = (bf16[2,256,256]{2,1,0:T(8,128)(2,1)S(1)}, bf16[2,256,256]{2,1,0:T(8,128)(2,1)}, u32[]{:S(2)}) copy-start(bf16[2,256,256]{2,1,0:T(8,128)(2,1)} %param.11) | copy-start | bytes 786436
  25.1 1.4 copy-start.2
  25.2 1.3 copy-start.9
  26.5 2.5 copy-start.14
  51.8 33.0 %all-to-all-start.2 = ((bf16[16,2,16,2048]{3,2,1,0:T(8,128)(2,1)}), bf16[16,2,16,2048]{3,2,1,0:T(8,128)(2,1)S(1)}, u32[]{:S(2)}, u32[]{:S(2)}) async-start(bf16[16,2,16,2048]{3,2,1,0:T(8,128)(2,1)} %copy.136), calls=%async_computation.2 | async-start | bytes 4194304 | tf_op jit(solution)/shard_map/all_to_all | solution.py:8
  84.8 17.2 %copy-start.11 = (bf16[16,2,16,2048]{3,2,1,0:T(8,128)(2,1)}, bf16[16,2,16,2048]{3,2,1,0:T(8,128)(2,1)S(1)}, u32[]{:S(2)}) copy-start(bf16[16,2,16,2048]{3,2,1,0:T(8,128)(2,1)S(1)} %all-to-all-done.2) | copy-start | bytes 6291460
  84.8 17.2 %copy-start.15 = (bf16[2,8,16,2,1024]{4,3,2,1,0:T(2,128)(2,1)S(1)}, bf16[2,8,16,2,1024]{4,3,2,1,0:T(2,128)(2,1)}, u32[]{:S(2)}) copy-start(bf16[2,8,16,2,1024]{4,3,2,1,0:T(2,128)(2,1)} %reshape.67) | copy-start | bytes 3145732
  110.3 35.0 %all-to-all-start.3 = ((bf16[16,2,16,2048]{3,2,1,0:T(8,128)(2,1)}), bf16[16,2,16,2048]{3,2,1,0:T(8,128)(2,1)S(1)}, u32[]{:S(2)}, u32[]{:S(2)}) async-start(bf16[16,2,16,2048]{3,2,1,0:T(8,128)(2,1)} %copy.139), calls=%async_computation.3 | async-start | bytes 4194304 | tf_op jit(solution)/shard_map/all_to_all | solution.py:8
  115.7 78.8 %reduce-scatter.2.cloned.1.call-start = ((), (), s32[]{:S(2)}) async-start(), calls=%async_computation.5 | async-start | bytes 1179648 | tf_op jit(solution)/shard_map/reduce_scatter | solution.py:68
  122.1 2.3 copy-start.12
  145.3 1.3 copy-start.4
  146.6 32.3 %all-to-all-start.1 = ((bf16[16,2,16,2048]{3,2,1,0:T(8,128)(2,1)}), bf16[16,2,16,2048]{3,2,1,0:T(8,128)(2,1)}, u32[]{:S(2)}, u32[]{:S(2)}) async-start(bf16[16,2,16,2048]{3,2,1,0:T(8,128)(2,1)} %copy.131), calls=%async_computation.1 | async-start | bytes 4194304 | tf_op jit(solution)/shard_map/all_to_all | solution.py:8
  151.5 94.3 %all-reduce.6.cloned.1.call-start = ((), (), s32[]{:S(2)}) async-start(), calls=%async_computation.6 | async-start | bytes 3145728
  151.6 8.8 %copy-start.5 = (bf16[16,2,16,2048]{3,2,1,0:T(8,128)(2,1)S(1)}, bf16[16,2,16,2048]{3,2,1,0:T(8,128)(2,1)}, u32[]{:S(2)}) copy-start(bf16[16,2,16,2048]{3,2,1,0:T(8,128)(2,1)} %copy-done.4) | copy-start | bytes 6291460
  158.3 2.1 copy-start.1
  160.4 18.5 %copy-start.3 = (bf16[2048,2,256]{2,1,0:T(2,128)(2,1)S(1)}, bf16[2048,2,256]{2,1,0:T(2,128)(2,1)}, u32[]{:S(2)}) copy-start(bf16[2048,2,256]{2,1,0:T(2,128)(2,1)} %copy-done.2) | copy-start | bytes 6291460
  178.9 4.7 %copy-start.8 = (bf16[2,256,256]{1,2,0:T(8,128)(2,1)S(1)}, bf16[2,256,256]{1,2,0:T(8,128)(2,1)}, u32[]{:S(2)}) copy-start(bf16[2,256,256]{1,2,0:T(8,128)(2,1)} %copy-done.7) | copy-start | bytes 786436
  181.2 1.1 copy-start.18
  181.2 2.3 copy-start.6
  185.6 4.0 %copy-start.10 = (bf16[2,8,16,2,256]{4,3,2,1,0:T(2,128)(2,1)S(1)}, bf16[2,8,16,2,256]{4,3,2,1,0:T(2,128)(2,1)}, u32[]{:S(2)}) copy-start(bf16[2,8,16,2,256]{4,3,2,1,0:T(2,128)(2,1)} %copy-done.9) | copy-start | bytes 786436
Sparse Core Ops, SparseCore 0:
  131.6 31.4 reduce-scatter.1
  182.4 63.3 all-reduce.5
where the time goes:
time: 258 us; the launch traced here: 256 us
  waiting for transfers between devices  117 us (45%)
  matrix products  63.7 us (25%)
  local copies, waits for them, and re-layouts  33.4 us (13%)
  starting transfers between devices  23.6 us (9%)
  between operations  15 us (6%)
  other arithmetic  3.75 us (1%)
    all_to_all x4, waiting for transfers between devices, permute(): lax.all_to_all(slots, 'tensor', split_axis=0, concat_axis=0, tiled=True)  67.4 us
    unnamed x3, waiting for transfers between devices  49.7 us
    all_to_all x4, starting transfers between devices, permute(): lax.all_to_all(slots, 'tensor', split_axis=0, concat_axis=0, tiled=True)  23.3 us
    dot_general x1, matrix products, shards(): jnp.einsum('qkpt,koqp->tko', back_down, third_view, preferred_element_typ...  17.2 us
    unnamed x46, local copies, waits for them, and re-layouts  13.8 us
    dot_general x1, matrix products, shards(): jnp.einsum('qakst,ksqao->tko', arrived_view, second_view, preferred_eleme...  13.5 us
    dot_general x1, matrix products, shards(): jnp.einsum('qakst,tko->ksqao', arrived_view, pre_grad, preferred_element_...  6.73 us
    unnamed x1, matrix products  5.76 us
  transfers between devices with their start and end apart: 6, of which 5 were waited for; matrix products, arithmetic and copies ran while one was open for 25% of the time, Pallas kernels for 0%

commit v1 on v0

v1 whole, which is shorter than its diff:
```python
import functools
import math

import jax
import jax.numpy as jnp
from jax import lax
from jax.experimental import pallas as pl
from jax.experimental.pallas import tpu as pltpu
from jax.sharding import PartitionSpec as P

F32 = jnp.float32
BF16 = jnp.bfloat16
CHUNKS = 4
TILE = 128
COEF = math.sqrt(2.0 / math.pi)
CUBE = 0.044715 * COEF


def dot(a, b):
    return lax.dot_general(a, b, (((1,), (0,)), ((), ())), preferred_element_type=F32)


def dot_nt(a, b):
    return lax.dot_general(a, b, (((1,), (1,)), ((), ())), preferred_element_type=F32)


def perm_in():
    i = lax.broadcasted_iota(jnp.int32, (256, 256), 0)
    j = lax.broadcasted_iota(jnp.int32, (256, 256), 1)
    return jnp.where((i & 7) * 32 + (i >> 3) == j, 1.0, 0.0).astype(BF16)


def perm_out():
    i = lax.broadcasted_iota(jnp.int32, (256, 256), 0)
    j = lax.broadcasted_iota(jnp.int32, (256, 256), 1)
    return jnp.where((i & 31) * 8 + (i >> 5) == j, 1.0, 0.0).astype(BF16)


def pack(dst, c, a, b):
    for q in range(16):
        lo = q * 16
        rows = [a[lo:lo + 8], b[lo:lo + 8], a[lo + 8:lo + 16], b[lo + 8:lo + 16]]
        dst[c, q] = jnp.concatenate(rows, axis=0).astype(BF16)


def kernel(scale,
           x_hbm, g_hbm, w1_hbm, w2_hbm, w3_hbm, w4_hbm,
           lo_hbm, tg_hbm, g1_hbm, g2_hbm, g3_hbm, g4_hbm,
           x, g, w1, w2, w3, w4, w1t, w2p, w2t, w3t, w4p,
           s1, s2, s3, s4, r1, r2, r3, r4, hid, pgr, md, bi,
           a1, a2, a3, a4, q1, q2, q3, q4, p1, p2, p3, p4,
           lo, tg, o1, o2, o3, o4,
           wsem, xsem, gsem, ssem, rsem, qsem, psem, osem):
    T = x.shape[0] // CHUNKS
    dp = lax.axis_index("dp")
    me = lax.axis_index("tensor")
    mz, mx = me // 4, me % 4

    def rows_of(c):
        return pl.ds(pl.multiple_of(c * T, T), T)

    loads = [
        pltpu.make_async_copy(h, v, wsem.at[i])
        for i, (h, v) in enumerate([(w1_hbm, w1), (w4_hbm, w4), (w2_hbm, w2), (w3_hbm, w3)])
    ]

    def load_x(c):
        return pltpu.make_async_copy(x_hbm.at[rows_of(c)], x.at[rows_of(c)], xsem.at[c])

    def load_g(c):
        return pltpu.make_async_copy(g_hbm.at[rows_of(c)], g.at[rows_of(c)], gsem.at[c])

    loads[0].start()
    load_x(0).start()
    loads[1].start()
    load_g(0).start()
    for c in range(1, CHUNKS):
        load_x(c).start()
        load_g(c).start()
    loads[2].start()
    loads[3].start()

    barrier = pltpu.get_barrier_semaphore()

    def greet_tensor(i, carry):
        pl.semaphore_signal(barrier, inc=1, device_id={"tensor": (me + i) % 16})
        return carry

    def greet_dp(i, carry):
        pl.semaphore_signal(barrier, inc=1, device_id={"dp": (dp + i) % 8})
        return carry

    lax.fori_loop(1, 16, greet_tensor, 0)
    lax.fori_loop(1, 8, greet_dp, 0)

    def send(n, src, dst, c):
        def one(i, carry):
            q = ((mz + i // 4) % 4) * 4 + (mx + i % 4) % 4
            pltpu.make_async_remote_copy(
                src_ref=src.at[c, q], dst_ref=dst.at[c, me],
                send_sem=ssem.at[n, c], recv_sem=rsem.at[n, c],
                device_id={"tensor": q},
            ).start()
            return carry

        pltpu.make_async_copy(src.at[c, me], dst.at[c, me], rsem.at[n, c]).start()
        lax.fori_loop(1, 16, one, 0)

    def arrive(n, dst, c):
        pltpu.make_async_copy(dst.at[c], dst.at[c], rsem.at[n, c]).wait()

    def sent(n, src, c):
        part = src.at[c, pl.ds(0, 15)]
        pltpu.make_async_copy(part, part, ssem.at[n, c]).wait()

    loads[0].wait()
    for b in range(2):
        w1t[b] = w1[b].T
    loads[1].wait()
    pin = perm_in()
    for b in range(2):
        w4p[b] = dot(pin, w4[b]).astype(BF16)

    pl.semaphore_wait(barrier, 22)

    def mix(c, carry):
        load_x(c).wait()
        a, b = (dot_nt(w1t[n], x[rows_of(c), n * 256:(n + 1) * 256]) for n in range(2))
        pack(s1, c, a, b)
        send(0, s1, r1, c)
        load_g(c).wait()
        a, b = (dot_nt(w4p[n], g[rows_of(c), n * 256:(n + 1) * 256]) for n in range(2))
        pack(s2, c, a, b)
        send(1, s2, r2, c)
        return carry

    lax.fori_loop(0, CHUNKS, mix, 0)

    loads[2].wait()
    loads[3].wait()
    for b in range(2):
        w2p[b] = dot(pin, w2[b]).astype(BF16)
        w2t[b] = w2p[b].T
        w3t[b] = w3[b].T
    a1[...] = jnp.zeros_like(a1)
    a2[...] = jnp.zeros_like(a2)
    a3[...] = jnp.zeros_like(a3)
    a4[...] = jnp.zeros_like(a4)

    def hidden_stage(c, carry):
        arrive(0, r1, c)
        arrive(1, r2, c)
        for k in range(2):
            arr = r1[c, :, k * 16:(k + 1) * 16, :].reshape(256, T)
            bd = r2[c, :, k * 16:(k + 1) * 16, :].reshape(256, T)

            def tile(n, inner):
                o = pl.ds(pl.multiple_of(n * TILE, TILE), TILE)
                v = dot(w2t[k, o, :], arr)
                hg = dot(w3[k, o, :], bd)
                v2 = v * v
                t = jnp.tanh(v * (COEF + CUBE * v2))
                h = 0.5 + 0.5 * t
                hid[o, :] = (v * h).astype(BF16)
                slope = h + (0.5 * v) * (1.0 - t * t) * (COEF + (3.0 * CUBE) * v2)
                pgr[o, :] = (slope * hg).astype(BF16)
                return inner

            lax.fori_loop(0, 1024 // TILE, tile, 0)
            md[k] = dot(w3t[k], hid[...])
            bi[k] = dot(w2p[k], pgr[...])
            a3[k] += dot_nt(hid[...], bd)
            a2[k] += dot_nt(pgr[...], arr)
        pack(s3, c, md[0], md[1])
        send(2, s3, r3, c)
        pack(s4, c, bi[0], bi[1])
        return carry

    lax.fori_loop(0, CHUNKS, hidden_stage, 0)

    def send_back(c, carry):
        send(3, s4, r4, c)
        return carry

    lax.fori_loop(0, CHUNKS, send_back, 0)

    def reduce_send(n, src, dst):
        def one(i, carry):
            p = (dp + i) % 8
            pltpu.make_async_remote_copy(
                src_ref=src.at[p], dst_ref=dst.at[dp],
                send_sem=qsem.at[n], recv_sem=psem.at[n],
                device_id={"dp": p},
            ).start()
            return carry

        pltpu.make_async_copy(src.at[dp], dst.at[dp], psem.at[n]).start()
        lax.fori_loop(1, 8, one, 0)

    def reduce_take(n, dst, out, out_hbm):
        pltpu.make_async_copy(dst, dst, psem.at[n]).wait()
        total = dst[0].astype(F32)
        for p in range(1, 8):
            total += dst[p].astype(F32)
        out[...] = total
        pltpu.make_async_copy(out, out_hbm, osem.at[n]).start()

    pout = perm_out()
    for k in range(2):
        for d in range(8):
            q3[d, k] = (a3[k, d * 128:(d + 1) * 128, :] * scale).astype(BF16)
    reduce_send(2, q3, p3)
    for k in range(2):
        full = dot_nt(pout, (a2[k] * scale).astype(BF16)).astype(BF16)
        for d in range(8):
            q2[d, k] = full[d * 32:(d + 1) * 32, :]
    reduce_send(1, q2, p2)

    def out_stage(c, carry):
        arrive(2, r3, c)
        rows = rows_of(c)
        for n in range(2):
            cols = slice(n * 256, (n + 1) * 256)
            ret = r3[c, :, n * 16:(n + 1) * 16, :].reshape(256, T)
            a4[n] += dot(ret, g[rows, cols])
            lo[rows, cols] = dot(ret.T, w4p[n]).astype(BF16)
        pltpu.make_async_copy(lo.at[rows], lo_hbm.at[rows], osem.at[4]).start()
        return carry

    lax.fori_loop(0, CHUNKS, out_stage, 0)
    for n in range(2):
        full = dot(pout, (a4[n] * scale).astype(BF16)).astype(BF16)
        for d in range(8):
            q4[d, n] = full[d * 32:(d + 1) * 32, :]
    reduce_send(3, q4, p4)
    reduce_take(2, p3, o3, g3_hbm)
    reduce_take(1, p2, o2, g2_hbm)

    def in_grads(c, carry):
        arrive(3, r4, c)
        rows = rows_of(c)
        for n in range(2):
            cols = slice(n * 256, (n + 1) * 256)
            ret = r4[c, :, n * 16:(n + 1) * 16, :].reshape(256, T)
            a1[n] += dot(ret, x[rows, cols])
            tg[rows, cols] = dot(ret.T, w1t[n]).astype(BF16)
        pltpu.make_async_copy(tg.at[rows], tg_hbm.at[rows], osem.at[5]).start()
        return carry

    lax.fori_loop(0, CHUNKS, in_grads, 0)
    for n in range(2):
        full = (a1[n] * scale).T.astype(BF16)
        for d in range(8):
            q1[d, n] = full[d * 32:(d + 1) * 32, :]
    reduce_send(0, q1, p1)
    reduce_take(3, p4, o4, g4_hbm)

    def drain(c, carry):
        for n, src in enumerate((s1, s2, s3, s4)):
            sent(n, src, c)
        return carry

    lax.fori_loop(0, CHUNKS, drain, 0)
    for n, src in enumerate((q1, q2, q3, q4)):
        if n:
            part = src.at[pl.ds(0, 7)]
            pltpu.make_async_copy(part, part, qsem.at[n]).wait()
    reduce_take(0, p1, o1, g1_hbm)
    part = q1.at[pl.ds(0, 7)]
    pltpu.make_async_copy(part, part, qsem.at[0]).wait()
    for n, (v, h) in enumerate([(o1, g1_hbm), (o2, g2_hbm), (o3, g3_hbm), (o4, g4_hbm), (lo, lo_hbm), (tg, tg_hbm)]):
        pltpu.make_async_copy(v, h, osem.at[n]).wait()


def shards(scale, tokens, cotangent, first, second, third, fourth):
    rows = tokens.shape[0]
    T = rows // CHUNKS
    slots = pltpu.VMEM((CHUNKS, 16, 32, T), BF16)
    any_spec = pl.BlockSpec(memory_space=pl.ANY)
    shape = jax.ShapeDtypeStruct
    grads = [(2, 32, 256), (2, 32, 1024), (2, 128, 256), (2, 32, 256)]
    return pl.pallas_call(
        functools.partial(kernel, scale),
        out_shape=[shape(tokens.shape, BF16), shape(tokens.shape, BF16)] + [shape(s, F32) for s in grads],
        in_specs=[any_spec] * 6,
        out_specs=[any_spec] * 6,
        scratch_shapes=[
            pltpu.VMEM(tokens.shape, BF16),
            pltpu.VMEM(tokens.shape, BF16),
            pltpu.VMEM(first.shape, BF16),
            pltpu.VMEM(second.shape, BF16),
            pltpu.VMEM(third.shape, BF16),
            pltpu.VMEM(fourth.shape, BF16),
            pltpu.VMEM((2, 256, 256), BF16),
            pltpu.VMEM((2, 256, 1024), BF16),
            pltpu.VMEM((2, 1024, 256), BF16),
            pltpu.VMEM((2, 256, 1024), BF16),
            pltpu.VMEM((2, 256, 256), BF16),
            slots, slots, slots, slots, slots, slots, slots, slots,
            pltpu.VMEM((1024, T), BF16),
            pltpu.VMEM((1024, T), BF16),
            pltpu.VMEM((2, 256, T), F32),
            pltpu.VMEM((2, 256, T), F32),
            pltpu.VMEM((2, 256, 256), F32),
            pltpu.VMEM((2, 1024, 256), F32),
            pltpu.VMEM((2, 1024, 256), F32),
            pltpu.VMEM((2, 256, 256), F32),
        ]
        + [pltpu.VMEM((8,) + s, BF16) for s in grads] * 2
        + [
            pltpu.VMEM(tokens.shape, BF16),
            pltpu.VMEM(tokens.shape, BF16),
        ]
        + [pltpu.VMEM(s, F32) for s in grads]
        + [
            pltpu.SemaphoreType.DMA((4,)),
            pltpu.SemaphoreType.DMA((CHUNKS,)),
            pltpu.SemaphoreType.DMA((CHUNKS,)),
            pltpu.SemaphoreType.DMA((4, CHUNKS)),
            pltpu.SemaphoreType.DMA((4, CHUNKS)),
            pltpu.SemaphoreType.DMA((4,)),
            pltpu.SemaphoreType.DMA((4,)),
            pltpu.SemaphoreType.DMA((6,)),
        ],
        compiler_params=pltpu.CompilerParams(
            collective_id=0, has_side_effects=True, vmem_limit_bytes=60 * 1024 * 1024
        ),
        cost_estimate=pl.CostEstimate(
            flops=16 * 10**9, bytes_accessed=12 * 2**20, transcendentals=4 * 2**20
        ),
    )(tokens, cotangent, first, second, third, fourth)


def solution(mesh):
    in_specs = (P("dp", "tensor"),) * 2 + (P("tensor", None, None),) * 4
    out_specs = (P("dp", "tensor"),) * 2 + (P("tensor", "dp", None),) * 4

    def run(tokens, *rest):
        scale = tokens.shape[0] ** -0.5
        step = jax.shard_map(
            functools.partial(shards, scale), mesh=mesh, in_specs=in_specs, out_specs=out_specs, check_vma=False
        )
        return step(tokens, *rest)

    return run
```

time: 258 us -> 116 us (0.45)
  waiting for transfers between devices: 117 us -> 0 us
  Pallas kernels: 0 us -> 108 us
  matrix products: 63.7 us -> 0 us
  local copies, waits for them, and re-layouts: 33.4 us -> 7.2 us
  starting transfers between devices: 23.6 us -> 0 us
  between operations: 15 us -> 0.67 us
  other arithmetic: 3.75 us -> 0 us
    pallas_call x0 -> x1, Pallas kernels: none -> 108 us  [shards(): pl.pallas_call(functools.partial(kernel, scale), out_shape=[shape(tokens....]
    all_to_all x4 -> x0, waiting for transfers between devices: 67.4 us -> none  [permute(): lax.all_to_all(slots, 'tensor', split_axis=0, concat_axis=0, tiled=True)]
    dot_general x11 -> x0, matrix products: 58 us -> none  [the longest x1 17.2 us: shards(): jnp.einsum('qkpt,koqp->tko', back_down, third_view, preferred_element_typ...]
    unnamed x3 -> x0, waiting for transfers between devices: 49.7 us -> none
    all_to_all x4 -> x0, starting transfers between devices: 23.3 us -> none  [permute(): lax.all_to_all(slots, 'tensor', split_axis=0, concat_axis=0, tiled=True)]
    reshape x6 -> x0, local copies, waits for them, and re-layouts: 11.4 us -> none  [the longest x1 2.59 us: shards(): inputs = tokens.reshape(row_count, local_blocks, block_width)]
    convert_element_type x6 -> x0, local copies, waits for them, and re-layouts: 8.17 us -> none  [the longest x1 2.08 us: shards(): second_part.astype(jnp.bfloat16)]
    unnamed x46 -> x16, local copies, waits for them, and re-layouts: 13.8 us -> 7.2 us
  transfers between devices with their start and end apart: 6 -> 0, of which waited for: 5 -> 0; matrix products, arithmetic and copies ran while one was open for 25% -> 0% of each run, Pallas kernels for 0% -> 0%
where the time goes in v1:
time: 116 us
  Pallas kernels  108 us (93%)
  local copies, waits for them, and re-layouts  7.2 us (6%)
    pallas_call x1, Pallas kernels, shards(): pl.pallas_call(functools.partial(kernel, scale), out_shape=[shape(tokens....  108 us
    unnamed x16, local copies, waits for them, and re-layouts  7.2 us

profile of v1, /device:TPU:1, one launch (start us, length us, event | category | flops | bytes accessed | tf_op | source)
XLA Modules:
  0.0 116.2 jit_solution(10986563498759365697)
XLA Ops:
  0.6 108.3 %shard_map.109 = (bf16[2048,512]{1,0:T(8,128)(2,1)}, bf16[2048,512]{1,0:T(8,128)(2,1)}, f32[2,32,256]{2,1,0:T(8,128)}, f32[2,32,1024]{2,1,0:T(8,128)}, f32[2,128,256]{2,1,0:T(8,128)}, /*index=5*/f32[2,32,256]{2,1,0:T(8,128)}) custom-call(bf16[2048,512]{1,0:T(8,128)(2,1)} %x_hbm.1, bf16[2048,512]{1,0:T(8,128)(2,1)} %g_hbm.1, bf16[2,256,256]{2,1,0:T(8,128)(2,1)} %w1_hbm.1, ...), custom_call_target="tpu_custom_call" | custom-call | flops 16000000000 | bytes 12582912 | tf_op jit(solution)/shard_map/pallas_call | solution.py:282
  109.0 0.0 copy-start
  109.0 3.2 %copy.18 = bf16[2048,512]{1,0:T(8,128)(2,1)} copy(bf16[2048,512]{1,0:T(8,128)(2,1)} %get-tuple-element.12) | data formatting | bytes 4194304
  112.2 0.0 copy-done
  112.2 0.0 copy-start.4
  112.2 0.0 copy-start.2
  112.2 0.0 copy-start.1
  112.2 0.0 copy-start.3
  112.2 1.3 %copy.19 = bf16[2048,512]{1,0:T(8,128)(2,1)} copy(bf16[2048,512]{1,0:T(8,128)(2,1)S(1)} %copy-done) | data formatting | bytes 4194304
  113.5 0.0 copy-done.4
  113.5 0.6 copy.20
  114.2 0.0 copy-done.2
  114.2 0.7 copy.21
  114.9 0.0 copy-done.1
  114.9 0.7 copy.22
  115.6 0.0 copy-done.3
  115.6 0.6 copy.23
Async XLA Ops:
  109.0 3.2 %copy-start = (bf16[2048,512]{1,0:T(8,128)(2,1)S(1)}, bf16[2048,512]{1,0:T(8,128)(2,1)}, u32[]{:S(2)}) copy-start(bf16[2048,512]{1,0:T(8,128)(2,1)} %get-tuple-element.13) | copy-start | bytes 6291460
  112.2 1.3 %copy-start.4 = (f32[2,32,256]{2,1,0:T(8,128)S(1)}, f32[2,32,256]{2,1,0:T(8,128)}, u32[]{:S(2)}) copy-start(f32[2,32,256]{2,1,0:T(8,128)} %get-tuple-element.14) | copy-start | bytes 196612
  112.2 2.0 %copy-start.2 = (f32[2,32,1024]{2,1,0:T(8,128)S(1)}, f32[2,32,1024]{2,1,0:T(8,128)}, u32[]{:S(2)}) copy-start(f32[2,32,1024]{2,1,0:T(8,128)} %get-tuple-element.15) | copy-start | bytes 786436
  112.2 2.7 %copy-start.1 = (f32[2,128,256]{2,1,0:T(8,128)S(1)}, f32[2,128,256]{2,1,0:T(8,128)}, u32[]{:S(2)}) copy-start(f32[2,128,256]{2,1,0:T(8,128)} %get-tuple-element.16) | copy-start | bytes 786436
  112.2 3.4 %copy-start.3 = (f32[2,32,256]{2,1,0:T(8,128)S(1)}, f32[2,32,256]{2,1,0:T(8,128)}, u32[]{:S(2)}) copy-start(f32[2,32,256]{2,1,0:T(8,128)} %get-tuple-element.17) | copy-start | bytes 196612

commit v2 on v1

v2 whole, which is shorter than its diff:
```python
import functools
import math

import jax
import jax.numpy as jnp
from jax import lax
from jax.experimental import pallas as pl
from jax.experimental.pallas import tpu as pltpu
from jax.sharding import PartitionSpec as P

F32 = jnp.float32
BF16 = jnp.bfloat16
CHUNKS = 4
TILE = 128
ORDER = ((2, 2), (1, 0), (3, 0), (2, 1), (0, 3), (1, 2), (3, 1), (0, 2), (2, 3), (1, 1), (3, 2), (0, 1), (1, 3), (2, 0), (3, 3))
COEF = math.sqrt(2.0 / math.pi)
CUBE = 0.044715 * COEF


def dot(a, b):
    return lax.dot_general(a, b, (((1,), (0,)), ((), ())), preferred_element_type=F32)


def dot_nt(a, b):
    return lax.dot_general(a, b, (((1,), (1,)), ((), ())), preferred_element_type=F32)


def perm_in():
    i = lax.broadcasted_iota(jnp.int32, (256, 256), 0)
    j = lax.broadcasted_iota(jnp.int32, (256, 256), 1)
    return jnp.where((i & 7) * 32 + (i >> 3) == j, 1.0, 0.0).astype(BF16)


def perm_out():
    i = lax.broadcasted_iota(jnp.int32, (256, 256), 0)
    j = lax.broadcasted_iota(jnp.int32, (256, 256), 1)
    return jnp.where((i & 31) * 8 + (i >> 5) == j, 1.0, 0.0).astype(BF16)


def pack(slot, a, b):
    for q in range(16):
        lo = q * 16
        rows = [a[lo:lo + 8], b[lo:lo + 8], a[lo + 8:lo + 16], b[lo + 8:lo + 16]]
        slot(q)[...] = jnp.concatenate(rows, axis=0).astype(BF16)


def kernel(scale,
           x_hbm, g_hbm, w1_hbm, w2_hbm, w3_hbm, w4_hbm,
           lo, tg, o1, o2, o3, o4,
           x, g, w1, w2, w3, w4, w1t, w2p, w2t, w3t, w4p, xt,
           s_in, r_in, s_md, r_md, s_bi, r_bi, s_end, r_end, hid, pgr, md, bi,
           a1, a2, a3, a4, q1, q2, q3, q4, p1, p2, p3, p4,
           wsem, xsem, gsem, in_sem, md_sem, bi_sem, end_sem, qsem, psem):
    T = x.shape[0] // CHUNKS
    dp = lax.axis_index("dp")
    me = lax.axis_index("tensor")
    mz, mx = me // 4, me % 4
    core = dp % 2
    turn = 1 - 2 * core

    def rows_of(c):
        return pl.ds(pl.multiple_of(c * T, T), T)

    loads = [
        pltpu.make_async_copy(h, v, wsem.at[i])
        for i, (h, v) in enumerate([(w1_hbm, w1), (w4_hbm, w4), (w2_hbm, w2), (w3_hbm, w3)])
    ]

    def load_x(c):
        return pltpu.make_async_copy(x_hbm.at[rows_of(c)], x.at[rows_of(c)], xsem.at[c])

    def load_g(c):
        return pltpu.make_async_copy(g_hbm.at[rows_of(c)], g.at[rows_of(c)], gsem.at[c])

    loads[0].start()
    load_x(0).start()
    loads[1].start()
    load_g(0).start()

    barrier = pltpu.get_barrier_semaphore()

    def greet_tensor(i, carry):
        pl.semaphore_signal(barrier, inc=1, device_id={"tensor": (me + i) % 16})
        return carry

    def greet_dp(i, carry):
        pl.semaphore_signal(barrier, inc=1, device_id={"dp": (dp + i) % 8})
        return carry

    lax.fori_loop(1, 16, greet_tensor, 0)
    lax.fori_loop(1, 8, greet_dp, 0)
    for c in range(1, CHUNKS):
        load_x(c).start()
        load_g(c).start()
    loads[2].start()
    loads[3].start()

    def send(sems, view, src, dst):
        pltpu.make_async_copy(view(src, me), view(dst, me), sems.at[1]).start()
        for dx, dz in ORDER:
            ax = (dx + core * (dz - dx)) * turn
            az = (dz + core * (dx - dz)) * turn
            q = ((mz + az + 4) % 4) * 4 + (mx + ax + 4) % 4
            pltpu.make_async_remote_copy(
                src_ref=view(src, q), dst_ref=view(dst, me),
                send_sem=sems.at[0], recv_sem=sems.at[1],
                device_id={"tensor": q},
            ).start()

    def arrive(sems, dst):
        pltpu.make_async_copy(dst, dst, sems.at[1]).wait()

    def sent(sems, src):
        part = src.at[pl.ds(0, 15)]
        pltpu.make_async_copy(part, part, sems.at[0]).wait()

    def mix_x(c):
        load_x(c).wait()
        a, b = (dot_nt(w1t[n], x[rows_of(c), n * 256:(n + 1) * 256]) for n in range(2))
        pack(lambda q: s_in.at[c, q, 0], a, b)

    def mix_g(c):
        load_g(c).wait()
        a, b = (dot_nt(w4p[n], g[rows_of(c), n * 256:(n + 1) * 256]) for n in range(2))
        pack(lambda q: s_in.at[c, q, 1], a, b)

    loads[0].wait()
    for b in range(2):
        w1t[b] = w1[b].T
    mix_x(0)
    pl.semaphore_wait(barrier, 22)
    send(in_sem.at[0], lambda ref, q: ref.at[0, q, 0], s_in, r_in)
    loads[1].wait()
    pin = perm_in()
    for b in range(2):
        w4p[b] = dot(pin, w4[b]).astype(BF16)
    mix_g(0)
    send(in_sem.at[0], lambda ref, q: ref.at[0, q, 1], s_in, r_in)

    def mix(c, carry):
        mix_x(c)
        mix_g(c)
        send(in_sem.at[c], lambda ref, q: ref.at[c, q], s_in, r_in)
        return carry

    lax.fori_loop(1, CHUNKS, mix, 0)

    loads[2].wait()
    loads[3].wait()
    for b in range(2):
        w2p[b] = dot(pin, w2[b]).astype(BF16)
        w2t[b] = w2p[b].T
        w3t[b] = w3[b].T
    a1[...] = jnp.zeros_like(a1)
    a2[...] = jnp.zeros_like(a2)
    a3[...] = jnp.zeros_like(a3)
    a4[...] = jnp.zeros_like(a4)

    def hidden_stage(c, pair):
        arrive(in_sem.at[c], r_in.at[c])
        for k in range(2):
            arr = r_in[c, :, 0, k * 16:(k + 1) * 16, :].reshape(256, T)
            bd = r_in[c, :, 1, k * 16:(k + 1) * 16, :].reshape(256, T)

            def tile(n, inner):
                o = pl.ds(pl.multiple_of(n * TILE, TILE), TILE)
                v = dot(w2t[k, o, :], arr)
                hg = dot(w3[k, o, :], bd)
                v2 = v * v
                t = jnp.tanh(v * (COEF + CUBE * v2))
                h = 0.5 + 0.5 * t
                hid[o, :] = (v * h).astype(BF16)
                slope = h + (0.5 * v) * (1.0 - t * t) * (COEF + (3.0 * CUBE) * v2)
                pgr[o, :] = (slope * hg).astype(BF16)
                return inner

            lax.fori_loop(0, 1024 // TILE, tile, 0)
            md[k] = dot(w3t[k], hid[...])
            bi[k] = dot(w2p[k], pgr[...])
            a3[k] += dot_nt(hid[...], bd)
            a2[k] += dot_nt(pgr[...], arr)
        half = c % 2
        pack(lambda q: s_md.at[pair, q, half], md[0], md[1])

        @pl.when(pair == 0)
        def _():
            pack(lambda q: s_bi.at[q, half], bi[0], bi[1])

        @pl.when(pair == 1)
        def _():
            pack(lambda q: s_end.at[half, q], bi[0], bi[1])

        return pair

    def hidden_pair(pair, carry):
        lax.fori_loop(2 * pair, 2 * pair + 2, hidden_stage, pair)
        send(md_sem.at[pair], lambda ref, q: ref.at[pair, q], s_md, r_md)

        @pl.when(pair == 0)
        def _():
            send(bi_sem, lambda ref, q: ref.at[q], s_bi, r_bi)

        return carry

    lax.fori_loop(0, 2, hidden_pair, 0)
    for half in range(2):
        send(end_sem.at[half], lambda ref, q: ref.at[half, q], s_end, r_end)

    def reduce_send(n, src, dst):
        def one(i, carry):
            p = (dp + i) % 8
            pltpu.make_async_remote_copy(
                src_ref=src.at[p], dst_ref=dst.at[dp],
                send_sem=qsem.at[n], recv_sem=psem.at[n],
                device_id={"dp": p},
            ).start()
            return carry

        pltpu.make_async_copy(src.at[dp], dst.at[dp], psem.at[n]).start()
        lax.fori_loop(1, 8, one, 0)

    def reduce_sent(n, src):
        part = src.at[pl.ds(0, 7)]
        pltpu.make_async_copy(part, part, qsem.at[n]).wait()

    def reduce_take(n, dst, out):
        pltpu.make_async_copy(dst, dst, psem.at[n]).wait()
        total = dst[0].astype(F32)
        for p in range(1, 8):
            total += dst[p].astype(F32)
        out[...] = total

    pout = perm_out()
    for k in range(2):
        for d in range(8):
            q3[d, k] = (a3[k, d * 128:(d + 1) * 128, :] * scale).astype(BF16)
    reduce_send(2, q3, p3)
    for k in range(2):
        full = dot_nt(pout, (a2[k] * scale).astype(BF16)).astype(BF16)
        for d in range(8):
            q2[d, k] = full[d * 32:(d + 1) * 32, :]
    reduce_send(1, q2, p2)

    def turn_x(c, carry):
        for n in range(2):
            xt[c, n] = x[rows_of(c), n * 256:(n + 1) * 256].T
        return carry

    lax.fori_loop(0, CHUNKS, turn_x, 0)

    def out_stage(c, pair):
        rows = rows_of(c)
        for n in range(2):
            cols = slice(n * 256, (n + 1) * 256)
            ret = r_md[pair, :, c % 2, n * 16:(n + 1) * 16, :].reshape(256, T)
            a4[n] += dot(ret, g[rows, cols])
            lo[rows, cols] = dot(ret.T, w4p[n]).astype(BF16)
        return pair

    def first_part(c, n, ret):
        a1[n] += dot_nt(xt[c, n], ret)

    def tokens_part(c, n, ret):
        tg[rows_of(c), n * 256:(n + 1) * 256] = dot(ret.T, w1t[n]).astype(BF16)

    def in_stage(c, carry):
        for n in range(2):
            ret = r_bi[:, c, n * 16:(n + 1) * 16, :].reshape(256, T)
            first_part(c, n, ret)
            tokens_part(c, n, ret)
        return carry

    arrive(md_sem.at[0], r_md.at[0])
    lax.fori_loop(0, 2, out_stage, 0)
    arrive(bi_sem, r_bi)
    lax.fori_loop(0, 2, in_stage, 0)
    reduce_take(2, p3, o3)
    reduce_take(1, p2, o2)
    arrive(md_sem.at[1], r_md.at[1])
    lax.fori_loop(2, 4, out_stage, 1)
    for n in range(2):
        full = dot(pout, (a4[n] * scale).astype(BF16)).astype(BF16)
        for d in range(8):
            q4[d, n] = full[d * 32:(d + 1) * 32, :]
    reduce_send(3, q4, p4)

    def ended(half, n):
        return r_end[half, :, n * 16:(n + 1) * 16, :].reshape(256, T)

    arrive(end_sem.at[0], r_end.at[0])
    for n in range(2):
        first_part(2, n, ended(0, n))
        tokens_part(2, n, ended(0, n))
    reduce_take(3, p4, o4)
    arrive(end_sem.at[1], r_end.at[1])
    for n in range(2):
        full = ((a1[n] + dot_nt(xt[3, n], ended(1, n))) * scale).astype(BF16)
        for d in range(8):
            q1[d, n] = full[d * 32:(d + 1) * 32, :]
    reduce_send(0, q1, p1)
    for n in range(2):
        tokens_part(3, n, ended(1, n))

    for c in range(CHUNKS):
        sent(in_sem.at[c], s_in.at[c])
    for pair in range(2):
        sent(md_sem.at[pair], s_md.at[pair])
        sent(end_sem.at[pair], s_end.at[pair])
    sent(bi_sem, s_bi)
    for n, src in enumerate((q1, q2, q3, q4)):
        reduce_sent(n, src)
    reduce_take(0, p1, o1)


def finish(*refs):
    sems = refs[-1]
    copies = [pltpu.make_async_copy(refs[n], refs[n + 6], sems.at[n]) for n in range(6)]
    for copy in copies:
        copy.start()
    for copy in copies:
        copy.wait()


def shards(scale, tokens, cotangent, first, second, third, fourth):
    rows = tokens.shape[0]
    T = rows // CHUNKS
    any_spec = pl.BlockSpec(memory_space=pl.ANY)
    shape = jax.ShapeDtypeStruct
    grads = [(2, 32, 256), (2, 32, 1024), (2, 128, 256), (2, 32, 256)]
    outs = [(tokens.shape, BF16), (tokens.shape, BF16)] + [(s, F32) for s in grads]
    parts = pl.pallas_call(
        functools.partial(kernel, scale),
        out_shape=[pltpu.VMEM(s, d) for s, d in outs],
        in_specs=[any_spec] * 6,
        out_specs=[pl.BlockSpec(memory_space=pltpu.VMEM)] * 6,
        scratch_shapes=[
            pltpu.VMEM(tokens.shape, BF16),
            pltpu.VMEM(tokens.shape, BF16),
            pltpu.VMEM(first.shape, BF16),
            pltpu.VMEM(second.shape, BF16),
            pltpu.VMEM(third.shape, BF16),
            pltpu.VMEM(fourth.shape, BF16),
            pltpu.VMEM((2, 256, 256), BF16),
            pltpu.VMEM((2, 256, 1024), BF16),
            pltpu.VMEM((2, 1024, 256), BF16),
            pltpu.VMEM((2, 256, 1024), BF16),
            pltpu.VMEM((2, 256, 256), BF16),
            pltpu.VMEM((CHUNKS, 2, 256, T), BF16),
            pltpu.VMEM((CHUNKS, 16, 2, 32, T), BF16),
            pltpu.VMEM((CHUNKS, 16, 2, 32, T), BF16),
            pltpu.VMEM((2, 16, 2, 32, T), BF16),
            pltpu.VMEM((2, 16, 2, 32, T), BF16),
            pltpu.VMEM((16, 2, 32, T), BF16),
            pltpu.VMEM((16, 2, 32, T), BF16),
            pltpu.VMEM((2, 16, 32, T), BF16),
            pltpu.VMEM((2, 16, 32, T), BF16),
            pltpu.VMEM((1024, T), BF16),
            pltpu.VMEM((1024, T), BF16),
            pltpu.VMEM((2, 256, T), F32),
            pltpu.VMEM((2, 256, T), F32),
            pltpu.VMEM((2, 256, 256), F32),
            pltpu.VMEM((2, 1024, 256), F32),
            pltpu.VMEM((2, 1024, 256), F32),
            pltpu.VMEM((2, 256, 256), F32),
        ]
        + [pltpu.VMEM((8,) + s, BF16) for s in grads] * 2
        + [
            pltpu.SemaphoreType.DMA((4,)),
            pltpu.SemaphoreType.DMA((CHUNKS,)),
            pltpu.SemaphoreType.DMA((CHUNKS,)),
            pltpu.SemaphoreType.DMA((CHUNKS, 2)),
            pltpu.SemaphoreType.DMA((2, 2)),
            pltpu.SemaphoreType.DMA((2,)),
            pltpu.SemaphoreType.DMA((2, 2)),
            pltpu.SemaphoreType.DMA((4,)),
            pltpu.SemaphoreType.DMA((4,)),
        ],
        compiler_params=pltpu.CompilerParams(
            collective_id=0, has_side_effects=True, vmem_limit_bytes=48 * 1024 * 1024
        ),
        cost_estimate=pl.CostEstimate(
            flops=16 * 10**9, bytes_accessed=12 * 2**20, transcendentals=4 * 2**20
        ),
    )(*(pltpu.with_memory_space_constraint(a, pltpu.HBM) for a in (tokens, cotangent, first, second, third, fourth)))
    return pl.pallas_call(
        finish,
        out_shape=[shape(s, d) for s, d in outs],
        in_specs=[pl.BlockSpec(memory_space=pltpu.VMEM)] * 6,
        out_specs=[any_spec] * 6,
        scratch_shapes=[pltpu.SemaphoreType.DMA((6,))],
        compiler_params=pltpu.CompilerParams(vmem_limit_bytes=1024 * 1024),
    )(*parts)


def solution(mesh):
    in_specs = (P("dp", "tensor"),) * 2 + (P("tensor", None, None),) * 4
    out_specs = (P("dp", "tensor"),) * 2 + (P("tensor", "dp", None),) * 4

    def run(tokens, *rest):
        scale = tokens.shape[0] ** -0.5
        step = jax.shard_map(
            functools.partial(shards, scale), mesh=mesh, in_specs=in_specs, out_specs=out_specs, check_vma=False
        )
        return step(tokens, *rest)

    return run
```

time: 116 us -> 110 us (0.948)
  local copies, waits for them, and re-layouts: 7.2 us -> 0 us
    unnamed x16 -> x0, local copies, waits for them, and re-layouts: 7.2 us -> none
    pallas_call x1 -> x2, Pallas kernels: 108 us -> 109 us  [the longest x1 107 us: shards(): pl.pallas_call(functools.partial(kernel, scale), out_shape=[pltpu.VMEM(s,...]
where the time goes in v2:
time: 110 us
  Pallas kernels  109 us (99%)
    pallas_call x1, Pallas kernels, shards(): pl.pallas_call(functools.partial(kernel, scale), out_shape=[pltpu.VMEM(s,...  107 us
    pallas_call x1, Pallas kernels, shards(): pl.pallas_call(finish, out_shape=[shape(s, d) for s, d in outs], in_specs...  2.24 us

profile of v2, /device:TPU:1, one launch (start us, length us, event | category | flops | bytes accessed | tf_op | source)
XLA Modules:
  0.0 109.7 jit_solution(5822339874096284051)
XLA Ops:
  0.6 106.8 %shard_map.109 = (bf16[2048,512]{1,0:T(8,128)(2,1)S(1)}, bf16[2048,512]{1,0:T(8,128)(2,1)S(1)}, f32[2,32,256]{2,1,0:T(8,128)S(1)}, f32[2,32,1024]{2,1,0:T(8,128)...) custom-call(bf16[2048,512]{1,0:T(8,128)(2,1)} %x_hbm.1, bf16[2048,512]{1,0:T(8,128)(2,1)} %g_hbm.1, ...), custom_call_target="tpu_custom_call" | custom-call | flops 16000000000 | bytes 12582912 | tf_op jit(solution)/shard_map/pallas_call | solution.py:331
  107.4 2.2 %shard_map.110 = (bf16[2048,512]{1,0:T(8,128)(2,1)}, bf16[2048,512]{1,0:T(8,128)(2,1)}, f32[2,32,256]{2,1,0:T(8,128)}, f32[2,32,1024]{2,1,0:T(8,128)}, f32[2,128,256]{2,1,0:T(8,128)}, /*index=5*/f32[2,32,256]{2,1,0:T(8,128)}) custom-call(bf16[2048,512]{1,0:T(8,128)(2,1)S(1)} %get-tuple-element.12.refs_0_, bf16[2048,512]{1,0:T(8,128)(2,1)S(1)} %get-tuple-element.13.refs_1_, ...), custom_call_target="tpu_custom_call" | custom-call | tf_op jit(solution)/shard_map/pallas_call | solution.py:385

commit v3 on v2

--- a/solution.py
+++ b/solution.py
@@ -12,7 +12,7 @@
 BF16 = jnp.bfloat16
 CHUNKS = 4
 TILE = 128
-ORDER = ((2, 2), (1, 0), (3, 0), (2, 1), (0, 3), (1, 2), (3, 1), (0, 2), (2, 3), (1, 1), (3, 2), (0, 1), (1, 3), (2, 0), (3, 3))
+FAR = ((2, 2), (2, 1), (2, 3), (1, 2), (3, 2), (0, 2), (2, 0), (1, 1), (3, 3), (1, 3), (3, 1), (1, 0), (3, 0), (0, 1), (0, 3))
 COEF = math.sqrt(2.0 / math.pi)
 CUBE = 0.044715 * COEF
 
@@ -48,9 +48,9 @@
            x_hbm, g_hbm, w1_hbm, w2_hbm, w3_hbm, w4_hbm,
            lo, tg, o1, o2, o3, o4,
            x, g, w1, w2, w3, w4, w1t, w2p, w2t, w3t, w4p, xt,
-           s_in, r_in, s_md, r_md, s_bi, r_bi, s_end, r_end, hid, pgr, md, bi,
-           a1, a2, a3, a4, q1, q2, q3, q4, p1, p2, p3, p4,
-           wsem, xsem, gsem, in_sem, md_sem, bi_sem, end_sem, qsem, psem):
+           s_in, r_in, s_md, r_md, s_b0, r_b0, s_b1, r_b1, hid, pgr, md, bi,
+           a1, a2, a3, a4, q0, q1, q2, q3, q4, p0, p1, p2, p3, p4,
+           wsem, xsem, gsem, in_sem, md_sem, b0_sem, b1_sem, qsem, psem):
     T = x.shape[0] // CHUNKS
     dp = lax.axis_index("dp")
     me = lax.axis_index("tensor")
@@ -97,7 +97,7 @@
 
     def send(sems, view, src, dst):
         pltpu.make_async_copy(view(src, me), view(dst, me), sems.at[1]).start()
-        for dx, dz in ORDER:
+        for dx, dz in FAR:
             ax = (dx + core * (dz - dx)) * turn
             az = (dz + core * (dx - dz)) * turn
             q = ((mz + az + 4) % 4) * 4 + (mx + ax + 4) % 4
@@ -182,29 +182,22 @@
         half = c % 2
         pack(lambda q: s_md.at[pair, q, half], md[0], md[1])
 
-        @pl.when(pair == 0)
-        def _():
-            pack(lambda q: s_bi.at[q, half], bi[0], bi[1])
-
-        @pl.when(pair == 1)
-        def _():
-            pack(lambda q: s_end.at[half, q], bi[0], bi[1])
-
+        for q in range(16):
+            for n, dst in enumerate((s_b0, s_b1)):
+                low = q * 16 + n * 8
+                rows = [bi[0, low:low + 8], bi[1, low:low + 8]]
+                dst[pair, q, half] = jnp.concatenate(rows, axis=0).astype(BF16)
         return pair
 
     def hidden_pair(pair, carry):
         lax.fori_loop(2 * pair, 2 * pair + 2, hidden_stage, pair)
         send(md_sem.at[pair], lambda ref, q: ref.at[pair, q], s_md, r_md)
-
-        @pl.when(pair == 0)
-        def _():
-            send(bi_sem, lambda ref, q: ref.at[q], s_bi, r_bi)
-
+        send(b0_sem.at[pair], lambda ref, q: ref.at[pair, q], s_b0, r_b0)
         return carry
 
     lax.fori_loop(0, 2, hidden_pair, 0)
-    for half in range(2):
-        send(end_sem.at[half], lambda ref, q: ref.at[half, q], s_end, r_end)
+    for pair in range(2):
+        send(b1_sem.at[pair], lambda ref, q: ref.at[pair, q], s_b1, r_b1)
 
     def reduce_send(n, src, dst):
         def one(i, carry):
@@ -216,8 +209,8 @@
             ).start()
             return carry
 
+        lax.fori_loop(1, 8, one, 0)
         pltpu.make_async_copy(src.at[dp], dst.at[dp], psem.at[n]).start()
-        lax.fori_loop(1, 8, one, 0)
 
     def reduce_sent(n, src):
         part = src.at[pl.ds(0, 7)]
@@ -263,16 +256,18 @@
     def tokens_part(c, n, ret):
         tg[rows_of(c), n * 256:(n + 1) * 256] = dot(ret.T, w1t[n]).astype(BF16)
 
+    def back(r_b, c):
+        return r_b[c // 2, :, c % 2].reshape(256, T)
+
     def in_stage(c, carry):
-        for n in range(2):
-            ret = r_bi[:, c, n * 16:(n + 1) * 16, :].reshape(256, T)
-            first_part(c, n, ret)
-            tokens_part(c, n, ret)
+        ret = back(r_b0, c)
+        first_part(c, 0, ret)
+        tokens_part(c, 0, ret)
         return carry
 
     arrive(md_sem.at[0], r_md.at[0])
     lax.fori_loop(0, 2, out_stage, 0)
-    arrive(bi_sem, r_bi)
+    arrive(b0_sem.at[0], r_b0.at[0])
     lax.fori_loop(0, 2, in_stage, 0)
     reduce_take(2, p3, o3)
     reduce_take(1, p2, o2)
@@ -283,33 +278,35 @@
         for d in range(8):
             q4[d, n] = full[d * 32:(d + 1) * 32, :]
     reduce_send(3, q4, p4)
-
-    def ended(half, n):
-        return r_end[half, :, n * 16:(n + 1) * 16, :].reshape(256, T)
-
-    arrive(end_sem.at[0], r_end.at[0])
-    for n in range(2):
-        first_part(2, n, ended(0, n))
-        tokens_part(2, n, ended(0, n))
+    arrive(b0_sem.at[1], r_b0.at[1])
+    lax.fori_loop(2, 4, in_stage, 0)
+    full = (a1[0] * scale).astype(BF16)
+    for d in range(8):
+        q0[d] = full[d * 32:(d + 1) * 32, :]
+    reduce_send(4, q0, p0)
+    arrive(b1_sem.at[0], r_b1.at[0])
+    for c in range(2):
+        first_part(c, 1, back(r_b1, c))
+        tokens_part(c, 1, back(r_b1, c))
     reduce_take(3, p4, o4)
-    arrive(end_sem.at[1], r_end.at[1])
-    for n in range(2):
-        full = ((a1[n] + dot_nt(xt[3, n], ended(1, n))) * scale).astype(BF16)
-        for d in range(8):
-            q1[d, n] = full[d * 32:(d + 1) * 32, :]
+    reduce_take(4, p0, o1.at[0])
+    arrive(b1_sem.at[1], r_b1.at[1])
+    full = a1[1] + dot_nt(xt[2, 1], back(r_b1, 2)) + dot_nt(xt[3, 1], back(r_b1, 3))
+    full = (full * scale).astype(BF16)
+    for d in range(8):
+        q1[d] = full[d * 32:(d + 1) * 32, :]
     reduce_send(0, q1, p1)
-    for n in range(2):
-        tokens_part(3, n, ended(1, n))
-
+    for c in range(2, 4):
+        tokens_part(c, 1, back(r_b1, c))
     for c in range(CHUNKS):
         sent(in_sem.at[c], s_in.at[c])
     for pair in range(2):
         sent(md_sem.at[pair], s_md.at[pair])
-        sent(end_sem.at[pair], s_end.at[pair])
-    sent(bi_sem, s_bi)
-    for n, src in enumerate((q1, q2, q3, q4)):
+        sent(b0_sem.at[pair], s_b0.at[pair])
+        sent(b1_sem.at[pair], s_b1.at[pair])
+    for n, src in enumerate((q1, q2, q3, q4, q0)):
         reduce_sent(n, src)
-    reduce_take(0, p1, o1)
+    reduce_take(0, p1, o1.at[1])
 
 
 def finish(*refs):
@@ -327,6 +324,7 @@
     any_spec = pl.BlockSpec(memory_space=pl.ANY)
     shape = jax.ShapeDtypeStruct
     grads = [(2, 32, 256), (2, 32, 1024), (2, 128, 256), (2, 32, 256)]
+    sums = [(32, 256), (32, 256)] + grads[1:]
     outs = [(tokens.shape, BF16), (tokens.shape, BF16)] + [(s, F32) for s in grads]
     parts = pl.pallas_call(
         functools.partial(kernel, scale),
@@ -350,10 +348,10 @@
             pltpu.VMEM((CHUNKS, 16, 2, 32, T), BF16),
             pltpu.VMEM((2, 16, 2, 32, T), BF16),
             pltpu.VMEM((2, 16, 2, 32, T), BF16),
-            pltpu.VMEM((16, 2, 32, T), BF16),
-            pltpu.VMEM((16, 2, 32, T), BF16),
-            pltpu.VMEM((2, 16, 32, T), BF16),
-            pltpu.VMEM((2, 16, 32, T), BF16),
+            pltpu.VMEM((2, 16, 2, 16, T), BF16),
+            pltpu.VMEM((2, 16, 2, 16, T), BF16),
+            pltpu.VMEM((2, 16, 2, 16, T), BF16),
+            pltpu.VMEM((2, 16, 2, 16, T), BF16),
             pltpu.VMEM((1024, T), BF16),
             pltpu.VMEM((1024, T), BF16),
             pltpu.VMEM((2, 256, T), F32),
@@ -363,17 +361,17 @@
             pltpu.VMEM((2, 1024, 256), F32),
             pltpu.VMEM((2, 256, 256), F32),
         ]
-        + [pltpu.VMEM((8,) + s, BF16) for s in grads] * 2
+        + [pltpu.VMEM((8,) + s, BF16) for s in sums] * 2
         + [
             pltpu.SemaphoreType.DMA((4,)),
             pltpu.SemaphoreType.DMA((CHUNKS,)),
             pltpu.SemaphoreType.DMA((CHUNKS,)),
             pltpu.SemaphoreType.DMA((CHUNKS, 2)),
             pltpu.SemaphoreType.DMA((2, 2)),
-            pltpu.SemaphoreType.DMA((2,)),
             pltpu.SemaphoreType.DMA((2, 2)),
-            pltpu.SemaphoreType.DMA((4,)),
-            pltpu.SemaphoreType.DMA((4,)),
+            pltpu.SemaphoreType.DMA((2, 2)),
+            pltpu.SemaphoreType.DMA((5,)),
+            pltpu.SemaphoreType.DMA((5,)),
         ],
         compiler_params=pltpu.CompilerParams(
             collective_id=0, has_side_effects=True, vmem_limit_bytes=48 * 1024 * 1024

time: 110 us -> 108 us (0.982)
    pallas_call x1, Pallas kernels: 107 us -> 105 us  [shards(): pl.pallas_call(functools.partial(kernel, scale), out_shape=[pltpu.VMEM(s,...]
where the time goes in v3:
time: 108 us
  Pallas kernels  108 us (100%)
    pallas_call x1, Pallas kernels, shards(): pl.pallas_call(functools.partial(kernel, scale), out_shape=[pltpu.VMEM(s,...  105 us
    pallas_call x1, Pallas kernels, shards(): pl.pallas_call(finish, out_shape=[shape(s, d) for s, d in outs], in_specs...  2.24 us

profile of v3, /device:TPU:1, one launch (start us, length us, event | category | flops | bytes accessed | tf_op | source)
XLA Modules:
  0.0 108.3 jit_solution(14861745757535330390)
XLA Ops:
  0.6 105.4 %shard_map.109 = (bf16[2048,512]{1,0:T(8,128)(2,1)S(1)}, bf16[2048,512]{1,0:T(8,128)(2,1)S(1)}, f32[2,32,256]{2,1,0:T(8,128)S(1)}, f32[2,32,1024]{2,1,0:T(8,128)...) custom-call(bf16[2048,512]{1,0:T(8,128)(2,1)} %x_hbm.1, bf16[2048,512]{1,0:T(8,128)(2,1)} %g_hbm.1, ...), custom_call_target="tpu_custom_call" | custom-call | flops 16000000000 | bytes 12582912 | tf_op jit(solution)/shard_map/pallas_call | solution.py:329
  106.1 2.2 %shard_map.110 = (bf16[2048,512]{1,0:T(8,128)(2,1)}, bf16[2048,512]{1,0:T(8,128)(2,1)}, f32[2,32,256]{2,1,0:T(8,128)}, f32[2,32,1024]{2,1,0:T(8,128)}, f32[2,128,256]{2,1,0:T(8,128)}, /*index=5*/f32[2,32,256]{2,1,0:T(8,128)}) custom-call(bf16[2048,512]{1,0:T(8,128)(2,1)S(1)} %get-tuple-element.12.refs_0_, bf16[2048,512]{1,0:T(8,128)(2,1)S(1)} %get-tuple-element.13.refs_1_, ...), custom_call_target="tpu_custom_call" | custom-call | tf_op jit(solution)/shard_map/pallas_call | solution.py:383

commit v4 on v3

--- a/solution.py
+++ b/solution.py
@@ -13,6 +13,7 @@
 CHUNKS = 4
 TILE = 128
 FAR = ((2, 2), (2, 1), (2, 3), (1, 2), (3, 2), (0, 2), (2, 0), (1, 1), (3, 3), (1, 3), (3, 1), (1, 0), (3, 0), (0, 1), (0, 3))
+ROWS = ((2, 1), (2, 0), (1, 1), (3, 1), (1, 0), (3, 0), (0, 1))
 COEF = math.sqrt(2.0 / math.pi)
 CUBE = 0.044715 * COEF
 
@@ -72,23 +73,21 @@
     def load_g(c):
         return pltpu.make_async_copy(g_hbm.at[rows_of(c)], g.at[rows_of(c)], gsem.at[c])
 
+    def peer(dx, dz):
+        return {"tensor": ((mz + dz) % 4) * 4 + (mx + dx) % 4}
+
+    def other(dy, dc):
+        return {"dp": ((dp // 2 + dy) % 4) * 2 + (core + dc) % 2}
+
+    barrier = pltpu.get_barrier_semaphore()
+    for dx, dz in FAR:
+        pl.semaphore_signal(barrier, inc=1, device_id=peer(dx, dz))
+    for dy, dc in ROWS:
+        pl.semaphore_signal(barrier, inc=1, device_id=other(dy, dc))
     loads[0].start()
     load_x(0).start()
     loads[1].start()
     load_g(0).start()
-
-    barrier = pltpu.get_barrier_semaphore()
-
-    def greet_tensor(i, carry):
-        pl.semaphore_signal(barrier, inc=1, device_id={"tensor": (me + i) % 16})
-        return carry
-
-    def greet_dp(i, carry):
-        pl.semaphore_signal(barrier, inc=1, device_id={"dp": (dp + i) % 8})
-        return carry
-
-    lax.fori_loop(1, 16, greet_tensor, 0)
-    lax.fori_loop(1, 8, greet_dp, 0)
     for c in range(1, CHUNKS):
         load_x(c).start()
         load_g(c).start()
@@ -200,16 +199,13 @@
         send(b1_sem.at[pair], lambda ref, q: ref.at[pair, q], s_b1, r_b1)
 
     def reduce_send(n, src, dst):
-        def one(i, carry):
-            p = (dp + i) % 8
+        for dy, dc in ROWS:
+            p = other(dy, dc)
             pltpu.make_async_remote_copy(
-                src_ref=src.at[p], dst_ref=dst.at[dp],
+                src_ref=src.at[p["dp"]], dst_ref=dst.at[dp],
                 send_sem=qsem.at[n], recv_sem=psem.at[n],
-                device_id={"dp": p},
+                device_id=p,
             ).start()
-            return carry
-
-        lax.fori_loop(1, 8, one, 0)
         pltpu.make_async_copy(src.at[dp], dst.at[dp], psem.at[n]).start()
 
     def reduce_sent(n, src):

time: 108 us -> 108 us (level)
  no operation moved by 1% of the time
where the time goes in v4:
time: 108 us
  Pallas kernels  107 us (99%)
    pallas_call x1, Pallas kernels, shards(): pl.pallas_call(functools.partial(kernel, scale), out_shape=[pltpu.VMEM(s,...  105 us
    pallas_call x1, Pallas kernels, shards(): pl.pallas_call(finish, out_shape=[shape(s, d) for s, d in outs], in_specs...  2.24 us

profile of v4, /device:TPU:1, one launch (start us, length us, event | category | flops | bytes accessed | tf_op | source)
XLA Modules:
  0.0 107.6 jit_solution(13663563368190278246)
XLA Ops:
  0.6 104.7 %shard_map.109 = (bf16[2048,512]{1,0:T(8,128)(2,1)S(1)}, bf16[2048,512]{1,0:T(8,128)(2,1)S(1)}, f32[2,32,256]{2,1,0:T(8,128)S(1)}, f32[2,32,1024]{2,1,0:T(8,128)...) custom-call(bf16[2048,512]{1,0:T(8,128)(2,1)} %x_hbm.1, bf16[2048,512]{1,0:T(8,128)(2,1)} %g_hbm.1, ...), custom_call_target="tpu_custom_call" | custom-call | flops 16000000000 | bytes 12582912 | tf_op jit(solution)/shard_map/pallas_call | solution.py:325
  105.4 2.2 %shard_map.110 = (bf16[2048,512]{1,0:T(8,128)(2,1)}, bf16[2048,512]{1,0:T(8,128)(2,1)}, f32[2,32,256]{2,1,0:T(8,128)}, f32[2,32,1024]{2,1,0:T(8,128)}, f32[2,128,256]{2,1,0:T(8,128)}, /*index=5*/f32[2,32,256]{2,1,0:T(8,128)}) custom-call(bf16[2048,512]{1,0:T(8,128)(2,1)S(1)} %get-tuple-element.12.refs_0_, bf16[2048,512]{1,0:T(8,128)(2,1)S(1)} %get-tuple-element.13.refs_1_, ...), custom_call_target="tpu_custom_call" | custom-call | tf_op jit(solution)/shard_map/pallas_call | solution.py:379

commit v5 on v4

--- a/solution.py
+++ b/solution.py
@@ -47,16 +47,16 @@
 
 def kernel(scale,
            x_hbm, g_hbm, w1_hbm, w2_hbm, w3_hbm, w4_hbm,
-           lo, tg, o1, o2, o3, o4,
+           lo, tg, o1, o2, o3, o4, p1,
            x, g, w1, w2, w3, w4, w1t, w2p, w2t, w3t, w4p, xt,
            s_in, r_in, s_md, r_md, s_b0, r_b0, s_b1, r_b1, hid, pgr, md, bi,
-           a1, a2, a3, a4, q0, q1, q2, q3, q4, p0, p1, p2, p3, p4,
+           a1, a2, a3, a4, q0, q1, q2, q3, q4, p0, p2, p3, p4,
            wsem, xsem, gsem, in_sem, md_sem, b0_sem, b1_sem, qsem, psem):
     T = x.shape[0] // CHUNKS
     dp = lax.axis_index("dp")
     me = lax.axis_index("tensor")
-    mz, mx = me // 4, me % 4
-    core = dp % 2
+    mz, mx = lax.div(me, 4), lax.rem(me, 4)
+    row, core = lax.div(dp, 2), lax.rem(dp, 2)
     turn = 1 - 2 * core
 
     def rows_of(c):
@@ -74,10 +74,10 @@
         return pltpu.make_async_copy(g_hbm.at[rows_of(c)], g.at[rows_of(c)], gsem.at[c])
 
     def peer(dx, dz):
-        return {"tensor": ((mz + dz) % 4) * 4 + (mx + dx) % 4}
+        return {"tensor": lax.rem(mz + dz, 4) * 4 + lax.rem(mx + dx, 4)}
 
     def other(dy, dc):
-        return {"dp": ((dp // 2 + dy) % 4) * 2 + (core + dc) % 2}
+        return {"dp": lax.rem(row + dy, 4) * 2 + (core + dc * turn)}
 
     barrier = pltpu.get_barrier_semaphore()
     for dx, dz in FAR:
@@ -99,7 +99,7 @@
         for dx, dz in FAR:
             ax = (dx + core * (dz - dx)) * turn
             az = (dz + core * (dx - dz)) * turn
-            q = ((mz + az + 4) % 4) * 4 + (mx + ax + 4) % 4
+            q = lax.rem(mz + az + 4, 4) * 4 + lax.rem(mx + ax + 4, 4)
             pltpu.make_async_remote_copy(
                 src_ref=view(src, q), dst_ref=view(dst, me),
                 send_sem=sems.at[0], recv_sem=sems.at[1],
@@ -285,7 +285,15 @@
         first_part(c, 1, back(r_b1, c))
         tokens_part(c, 1, back(r_b1, c))
     reduce_take(3, p4, o4)
-    reduce_take(4, p0, o1.at[0])
+    reduce_take(4, p0, o1)
+    for c in range(CHUNKS):
+        sent(in_sem.at[c], s_in.at[c])
+    for pair in range(2):
+        sent(md_sem.at[pair], s_md.at[pair])
+        sent(b0_sem.at[pair], s_b0.at[pair])
+    sent(b1_sem.at[0], s_b1.at[0])
+    for n, src in ((1, q2), (2, q3), (3, q4), (4, q0)):
+        reduce_sent(n, src)
     arrive(b1_sem.at[1], r_b1.at[1])
     full = a1[1] + dot_nt(xt[2, 1], back(r_b1, 2)) + dot_nt(xt[3, 1], back(r_b1, 3))
     full = (full * scale).astype(BF16)
@@ -294,22 +302,21 @@
     reduce_send(0, q1, p1)
     for c in range(2, 4):
         tokens_part(c, 1, back(r_b1, c))
-    for c in range(CHUNKS):
-        sent(in_sem.at[c], s_in.at[c])
-    for pair in range(2):
-        sent(md_sem.at[pair], s_md.at[pair])
-        sent(b0_sem.at[pair], s_b0.at[pair])
-        sent(b1_sem.at[pair], s_b1.at[pair])
-    for n, src in enumerate((q1, q2, q3, q4, q0)):
-        reduce_sent(n, src)
-    reduce_take(0, p1, o1.at[1])
-
-
-def finish(*refs):
-    sems = refs[-1]
-    copies = [pltpu.make_async_copy(refs[n], refs[n + 6], sems.at[n]) for n in range(6)]
-    for copy in copies:
+    sent(b1_sem.at[1], s_b1.at[1])
+    reduce_sent(0, q1)
+    pltpu.make_async_copy(p1, p1, psem.at[0]).wait()
+
+
+def finish(lo, tg, o1, o2, o3, o4, p1, lo_hbm, tg_hbm, g1, g2, g3, g4, last, sems):
+    pairs = [(lo, lo_hbm), (tg, tg_hbm), (o2, g2), (o3, g3), (o4, g4), (o1, g1.at[0]), (last, g1.at[1])]
+    copies = [pltpu.make_async_copy(src, dst, sems.at[n]) for n, (src, dst) in enumerate(pairs)]
+    for copy in copies[:-1]:
         copy.start()
+    total = p1[0].astype(F32)
+    for p in range(1, 8):
+        total += p1[p].astype(F32)
+    last[...] = total
+    copies[-1].start()
     for copy in copies:
         copy.wait()
 
@@ -322,11 +329,12 @@
     grads = [(2, 32, 256), (2, 32, 1024), (2, 128, 256), (2, 32, 256)]
     sums = [(32, 256), (32, 256)] + grads[1:]
     outs = [(tokens.shape, BF16), (tokens.shape, BF16)] + [(s, F32) for s in grads]
+    kept = outs[:2] + [((32, 256), F32)] + outs[3:] + [((8, 32, 256), BF16)]
     parts = pl.pallas_call(
         functools.partial(kernel, scale),
-        out_shape=[pltpu.VMEM(s, d) for s, d in outs],
+        out_shape=[pltpu.VMEM(s, d) for s, d in kept],
         in_specs=[any_spec] * 6,
-        out_specs=[pl.BlockSpec(memory_space=pltpu.VMEM)] * 6,
+        out_specs=[pl.BlockSpec(memory_space=pltpu.VMEM)] * 7,
         scratch_shapes=[
             pltpu.VMEM(tokens.shape, BF16),
             pltpu.VMEM(tokens.shape, BF16),
@@ -357,7 +365,7 @@
             pltpu.VMEM((2, 1024, 256), F32),
             pltpu.VMEM((2, 256, 256), F32),
         ]
-        + [pltpu.VMEM((8,) + s, BF16) for s in sums] * 2
+        + [pltpu.VMEM((8,) + s, BF16) for s in sums + sums[:1] + sums[2:]]
         + [
             pltpu.SemaphoreType.DMA((4,)),
             pltpu.SemaphoreType.DMA((CHUNKS,)),
@@ -379,9 +387,9 @@
     return pl.pallas_call(
         finish,
         out_shape=[shape(s, d) for s, d in outs],
-        in_specs=[pl.BlockSpec(memory_space=pltpu.VMEM)] * 6,
+        in_specs=[pl.BlockSpec(memory_space=pltpu.VMEM)] * 7,
         out_specs=[any_spec] * 6,
-        scratch_shapes=[pltpu.SemaphoreType.DMA((6,))],
+        scratch_shapes=[pltpu.VMEM((32, 256), F32), pltpu.SemaphoreType.DMA((7,))],
         compiler_params=pltpu.CompilerParams(vmem_limit_bytes=1024 * 1024),
     )(*parts)
 

time: 108 us -> 108 us (level)
  no operation moved by 1% of the time
where the time goes in v5:
time: 108 us
  Pallas kernels  107 us (99%)
    pallas_call x1, Pallas kernels, shards(): pl.pallas_call(functools.partial(kernel, scale), out_shape=[pltpu.VMEM(s,...  105 us
    pallas_call x1, Pallas kernels, shards(): pl.pallas_call(finish, out_shape=[shape(s, d) for s, d in outs], in_specs...  2.25 us

profile of v5, /device:TPU:1, one launch (start us, length us, event | category | flops | bytes accessed | tf_op | source)
XLA Modules:
  0.0 107.6 jit_solution(16118932743363938215)
XLA Ops:
  0.6 104.7 %shard_map.109 = (bf16[2048,512]{1,0:T(8,128)(2,1)S(1)}, bf16[2048,512]{1,0:T(8,128)(2,1)S(1)}, f32[32,256]{1,0:T(8,128)S(1)}, f32[2,32,1024]{2,1,0:T(8,128)S(1)...) custom-call(bf16[2048,512]{1,0:T(8,128)(2,1)} %x_hbm.1, ...), custom_call_target="tpu_custom_call" | custom-call | flops 16000000000 | bytes 12582912 | tf_op jit(solution)/shard_map/pallas_call | solution.py:333
  105.4 2.2 %shard_map.110 = (bf16[2048,512]{1,0:T(8,128)(2,1)}, bf16[2048,512]{1,0:T(8,128)(2,1)}, f32[2,32,256]{2,1,0:T(8,128)}, f32[2,32,1024]{2,1,0:T(8,128)}, f32[2,128,256]{2,1,0:T(8,128)}, /*index=5*/f32[2,32,256]{2,1,0:T(8,128)}) custom-call(bf16[2048,512]{1,0:T(8,128)(2,1)S(1)} %get-tuple-element.13.lo, bf16[2048,512]{1,0:T(8,128)(2,1)S(1)} %get-tuple-element.14.tg, ...), custom_call_target="tpu_custom_call" | custom-call | tf_op jit(solution)/shard_map/pallas_call | solution.py:387

commit v6 on v4

--- a/solution.py
+++ b/solution.py
@@ -94,9 +94,10 @@
     loads[2].start()
     loads[3].start()
 
-    def send(sems, view, src, dst):
-        pltpu.make_async_copy(view(src, me), view(dst, me), sems.at[1]).start()
-        for dx, dz in FAR:
+    def send(sems, view, src, dst, order=FAR):
+        if FAR[0] in order:
+            pltpu.make_async_copy(view(src, me), view(dst, me), sems.at[1]).start()
+        for dx, dz in order:
             ax = (dx + core * (dz - dx)) * turn
             az = (dz + core * (dx - dz)) * turn
             q = ((mz + az + 4) % 4) * 4 + (mx + ax + 4) % 4
@@ -195,8 +196,9 @@
         return carry
 
     lax.fori_loop(0, 2, hidden_pair, 0)
-    for pair in range(2):
-        send(b1_sem.at[pair], lambda ref, q: ref.at[pair, q], s_b1, r_b1)
+    for order in (FAR[:5], FAR[5:11], FAR[11:]):
+        for pair in range(2):
+            send(b1_sem.at[pair], lambda ref, q: ref.at[pair, q], s_b1, r_b1, order)
 
     def reduce_send(n, src, dst):
         for dy, dc in ROWS:

time: 108 us -> 108 us (level)
  no operation moved by 1% of the time
where the time goes in v6:
time: 108 us
  Pallas kernels  107 us (99%)
    pallas_call x1, Pallas kernels, shards(): pl.pallas_call(functools.partial(kernel, scale), out_shape=[pltpu.VMEM(s,...  105 us
    pallas_call x1, Pallas kernels, shards(): pl.pallas_call(finish, out_shape=[shape(s, d) for s, d in outs], in_specs...  2.24 us

profile of v6, /device:TPU:1, one launch (start us, length us, event | category | flops | bytes accessed | tf_op | source)
XLA Modules:
  0.0 107.8 jit_solution(3883361767737535115)
XLA Ops:
  0.6 104.9 %shard_map.109 = (bf16[2048,512]{1,0:T(8,128)(2,1)S(1)}, bf16[2048,512]{1,0:T(8,128)(2,1)S(1)}, f32[2,32,256]{2,1,0:T(8,128)S(1)}, f32[2,32,1024]{2,1,0:T(8,128)...) custom-call(bf16[2048,512]{1,0:T(8,128)(2,1)} %x_hbm.1, bf16[2048,512]{1,0:T(8,128)(2,1)} %g_hbm.1, ...), custom_call_target="tpu_custom_call" | custom-call | flops 16000000000 | bytes 12582912 | tf_op jit(solution)/shard_map/pallas_call | solution.py:327
  105.6 2.2 %shard_map.110 = (bf16[2048,512]{1,0:T(8,128)(2,1)}, bf16[2048,512]{1,0:T(8,128)(2,1)}, f32[2,32,256]{2,1,0:T(8,128)}, f32[2,32,1024]{2,1,0:T(8,128)}, f32[2,128,256]{2,1,0:T(8,128)}, /*index=5*/f32[2,32,256]{2,1,0:T(8,128)}) custom-call(bf16[2048,512]{1,0:T(8,128)(2,1)S(1)} %get-tuple-element.12.refs_0_, bf16[2048,512]{1,0:T(8,128)(2,1)S(1)} %get-tuple-element.13.refs_1_, ...), custom_call_target="tpu_custom_call" | custom-call | tf_op jit(solution)/shard_map/pallas_call | solution.py:381

commit v7 on v4

--- a/solution.py
+++ b/solution.py
@@ -55,8 +55,8 @@
     T = x.shape[0] // CHUNKS
     dp = lax.axis_index("dp")
     me = lax.axis_index("tensor")
-    mz, mx = me // 4, me % 4
-    core = dp % 2
+    mz, mx = lax.div(me, 4), lax.rem(me, 4)
+    row, core = lax.div(dp, 2), lax.rem(dp, 2)
     turn = 1 - 2 * core
 
     def rows_of(c):
@@ -74,10 +74,10 @@
         return pltpu.make_async_copy(g_hbm.at[rows_of(c)], g.at[rows_of(c)], gsem.at[c])
 
     def peer(dx, dz):
-        return {"tensor": ((mz + dz) % 4) * 4 + (mx + dx) % 4}
+        return {"tensor": lax.rem(mz + dz, 4) * 4 + lax.rem(mx + dx, 4)}
 
     def other(dy, dc):
-        return {"dp": ((dp // 2 + dy) % 4) * 2 + (core + dc) % 2}
+        return {"dp": lax.rem(row + dy, 4) * 2 + (core + dc * turn)}
 
     barrier = pltpu.get_barrier_semaphore()
     for dx, dz in FAR:
@@ -99,7 +99,7 @@
         for dx, dz in FAR:
             ax = (dx + core * (dz - dx)) * turn
             az = (dz + core * (dx - dz)) * turn
-            q = ((mz + az + 4) % 4) * 4 + (mx + ax + 4) % 4
+            q = lax.rem(mz + az + 4, 4) * 4 + lax.rem(mx + ax + 4, 4)
             pltpu.make_async_remote_copy(
                 src_ref=view(src, q), dst_ref=view(dst, me),
                 send_sem=sems.at[0], recv_sem=sems.at[1],

time: 108 us -> 108 us (level)
  no operation moved by 1% of the time
where the time goes in v7:
time: 108 us
  Pallas kernels  107 us (99%)
    pallas_call x1, Pallas kernels, shards(): pl.pallas_call(functools.partial(kernel, scale), out_shape=[pltpu.VMEM(s,...  105 us
    pallas_call x1, Pallas kernels, shards(): pl.pallas_call(finish, out_shape=[shape(s, d) for s, d in outs], in_specs...  2.24 us

profile of v7, /device:TPU:1, one launch (start us, length us, event | category | flops | bytes accessed | tf_op | source)
XLA Modules:
  0.0 107.6 jit_solution(8542795326165161131)
XLA Ops:
  0.6 104.7 %shard_map.109 = (bf16[2048,512]{1,0:T(8,128)(2,1)S(1)}, bf16[2048,512]{1,0:T(8,128)(2,1)S(1)}, f32[2,32,256]{2,1,0:T(8,128)S(1)}, f32[2,32,1024]{2,1,0:T(8,128)...) custom-call(bf16[2048,512]{1,0:T(8,128)(2,1)} %x_hbm.1, bf16[2048,512]{1,0:T(8,128)(2,1)} %g_hbm.1, ...), custom_call_target="tpu_custom_call" | custom-call | flops 16000000000 | bytes 12582912 | tf_op jit(solution)/shard_map/pallas_call | solution.py:325
  105.4 2.2 %shard_map.110 = (bf16[2048,512]{1,0:T(8,128)(2,1)}, bf16[2048,512]{1,0:T(8,128)(2,1)}, f32[2,32,256]{2,1,0:T(8,128)}, f32[2,32,1024]{2,1,0:T(8,128)}, f32[2,128,256]{2,1,0:T(8,128)}, /*index=5*/f32[2,32,256]{2,1,0:T(8,128)}) custom-call(bf16[2048,512]{1,0:T(8,128)(2,1)S(1)} %get-tuple-element.12.refs_0_, bf16[2048,512]{1,0:T(8,128)(2,1)S(1)} %get-tuple-element.13.refs_1_, ...), custom_call_target="tpu_custom_call" | custom-call | tf_op jit(solution)/shard_map/pallas_call | solution.py:379
